TPU v7x, 32 devices: a whole 2x2x4 slice. The times are simulated.
32 devices in a mesh: grp: 4 (over x, core), shard: 8 (over z, y).
Axes of the slice: x: 2, y: 2, z: 4, core: 2. Of those that a mesh axis runs over, the one named last changes fastest.
Arguments:
- activations: bfloat16 [1, 6144, 5120], P(None, ('grp', 'shard')), may hold values from -6 to 6
- out_grads: bfloat16 [1, 6144, 5120], P(None, ('grp', 'shard')), may hold values from -0.15234375 to 0.15234375
- error: float32 [4, 5120, 1, 5120], P('grp', 'shard'), may hold values from -6 to 6
- q_start: float32 [1, 32, 5120], replicated, may hold values from -6 to 6
Outputs:
- update: float32 [5120, 1, 5120], P('shard')
- error_next: float32 [4, 5120, 1, 5120], P('grp', 'shard')
- factor: float32 [1, 32, 5120], replicated
All inputs are finite; a program needn't handle non-finite values.
Results may differ from a plain program's by a relative error of at most 0.0034.
Values may be sent and summed in bfloat16 or wider, within the bound.
A program may use at most 256 MiB of HBM per device.

v0:
```python
import jax
import jax.numpy as jnp
from jax import lax
from jax.sharding import PartitionSpec as P

ITERS = 2


def local(activations, out_grads, error, q_start):
    own_rows = error.shape[1]
    mats = activations.shape[0]
    tok_count = activations.shape[1]
    width = activations.shape[2]
    groups = lax.axis_size("grp")
    high = lax.Precision.HIGHEST
    input_cols = lax.all_to_all(activations, "shard", split_axis=2, concat_axis=1, tiled=True)
    piece = lax.all_gather(out_grads, "shard", axis=1, tiled=True)
    blocks = piece.shape[1] // tok_count
    mine = input_cols.reshape(mats, blocks, tok_count, own_rows)
    grads = piece.reshape(mats, blocks, tok_count, width)
    partial_sum = jnp.einsum("mkta,mktc->kamc", mine, grads, preferred_element_type=jnp.float32)
    rounded = lax.optimization_barrier(partial_sum.astype(jnp.bfloat16)).astype(jnp.float32)
    gradient = jnp.sum(rounded, axis=0)
    momentum = gradient + error[0]
    right = q_start
    for step in range(ITERS):
        left = jnp.einsum("rmc,mkc->rmk", momentum, right, precision=high)
        gathered = lax.all_gather(left, ("grp", "shard"), axis=0, tiled=True)
        whole_left = jnp.sum(gathered.reshape(groups, -1, mats, left.shape[2]), axis=0) / groups
        gram = jnp.einsum("rmk,rml->mkl", whole_left, whole_left, precision=high)
        left = lax.dynamic_slice_in_dim(whole_left, lax.axis_index("shard") * own_rows, own_rows, 0)
        lower = jnp.linalg.cholesky(gram)
        basis = jax.vmap(lambda tri, rhs: jax.scipy.linalg.solve_triangular(tri, rhs, lower=True))(
            lower, left.transpose(1, 2, 0)
        )
        right = jnp.einsum("mkr,rmc->mkc", basis, momentum, precision=high)
        right = lax.psum(right, ("grp", "shard")) / groups
    update = jnp.einsum("mkr,mkc->rmc", basis, right, precision=high)
    return (update, (momentum - update)[None], right)


def solution(mesh):
    in_specs = (
        P(None, ("grp", "shard"), None),
        P(None, ("grp", "shard"), None),
        P("grp", "shard", None, None),
        P(),
    )
    out_specs = (P("shard", None, None), P("grp", "shard", None, None), P())
    return jax.shard_map(local, mesh=mesh, in_specs=in_specs, out_specs=out_specs, check_vma=False)
```

profile of v0, /device:TPU:0, one launch (start us, length us, event | category | flops | bytes accessed | tf_op | source)
XLA Modules:
  0.0 874.9 jit_solution(9473510842554681719)
XLA Ops:
  7.2 0.7 all-gather.4.cloned.1.call-update
  7.9 11.3 %copy.24 = bf16[1,192,5120]{1,0,2:T(2,128)(2,1)} copy(bf16[1,192,5120]{2,1,0:T(8,128)(2,1)} %param.7) | data formatting | bytes 3932160 | tf_op args[0]
  19.2 0.5 broadcast.87
  19.7 29.2 %reduce.10 = bf16[5120,192]{1,0:T(8,128)(2,1)S(1)} reduce(bf16[5120,1,192]{2,1,0:T(2,128)(2,1)} %bitcast.115, bf16[]{:T(256)} %broadcast.87), dimensions={1}, to_apply=%bitcast.109.reduce_sub_computation | reduce | bytes 3932162
  49.0 4.8 reshape.206
  53.7 7.3 all-to-all-start
  61.0 27.1 %copy.27 = f32[1,640,1,5120]{1,3,2,0:T(8,128)} copy(f32[1,640,1,5120]{3,2,1,0:T(1,128)} %param.9) | data formatting | bytes 26214400 | tf_op args[2]
  88.2 50.8 %all-to-all-done = bf16[8,2,61440]{2,1,0:T(2,128)(2,1)S(1)} async-done(((bf16[8,2,61440]{2,1,0:T(2,128)(2,1)}), bf16[8,2,61440]{2,1,0:T(2,128)(2,1)S(1)}, u32[]{:S(2)}, u32[]{:S(2)}) %all-to-all-start) | async-done | bytes 1966112 | tf_op jit(solution)/shard_map/all_to_all | solution.py:16
  139.0 5.5 reshape.207
  144.5 3.0 copy.39
  147.5 2.4 copy.26
  149.9 111.7 %all-gather.4.cloned.1.call-done = bf16[1,1536,5120]{2,1,0:T(8,128)(2,1)} async-done(((bf16[1,192,5120]{2,1,0:T(8,128)(2,1)}), bf16[1,1536,5120]{2,1,0:T(8,128)(2,1)}) %all-gather.4.cloned.1.call-update) | async-done | bytes 15728656 | tf_op jit(solution)/shard_map/all_gather | solution.py:17
  261.6 27.1 %convert_bitcast_fusion = bf16[8,640,1,5120]{1,3,0,2:T(8,128)(2,1)} fusion(bf16[8,192,5120]{2,1,0:T(8,128)(2,1)} %bitcast.117, bf16[1,192,8,640]{3,1,2,0:T(8,128)(2,1)} %copy.26), kind=kOutput, calls=%fused_computation.1 | convolution fusion | flops 10092544000 | bytes 70123520 | tf_op jit(solution)/shard_map/mkta,mktc->kamc/dot_general | solution.py:21
  288.7 22.8 %convert_reduce_fusion = f32[640,5120]{0,1:T(8,128)} fusion(bf16[8,640,1,5120]{1,3,0,2:T(8,128)(2,1)} %convert_bitcast_fusion), kind=kLoop, calls=%fused_computation | loop fusion | flops 49152000 | bytes 65536000 | tf_op jit(solution)/shard_map/reduce_sum | solution.py:23
  311.5 9.7 %bitcast_add_fusion.1 = f32[1,640,1,5120]{1,3,2,0:T(8,128)S(1)} fusion(f32[1,640,1,5120]{1,3,2,0:T(8,128)} %copy.27, f32[640,5120]{0,1:T(8,128)} %convert_reduce_fusion), kind=kLoop, calls=%fused_computation.13 | loop fusion | flops 3276800 | bytes 39321600 | tf_op jit(solution)/shard_map/add | solution.py:24
  321.2 4.7 copy-done.1
  325.9 8.0 fusion.17
  333.9 56.5 %all-gather.6.cloned.1.call-done = f32[20480,1,32]{0,2,1:T(8,128)} async-done(((f32[640,1,32]{0,2,1:T(8,128)}), f32[20480,1,32]{0,2,1:T(8,128)}) %all-gather.6.cloned.1.call-update) | async-done | bytes 2621456 | tf_op jit(solution)/shard_map/all_gather | solution.py:28
  390.4 3.3 reshape.193
  393.7 2.5 reduce_sum.33
  396.2 2.1 fusion.45
  398.3 1.1 broadcast_multiply_fusion.2
  399.5 2.9 custom-call.8
  402.4 0.6 compare_reduce_fusion.1
  403.1 0.7 fusion.34
  403.7 2.4 custom-call.9
  406.2 0.3 fusion.30
  406.5 17.7 %fusion.10 = f32[1,32,5120]{2,1,0:T(8,128)} fusion(f32[32,640]{1,0:T(8,128)S(1)} %fusion.30, f32[1,640,1,5120]{1,3,2,0:T(8,128)} %copy-done.1), kind=kOutput, calls=%fused_computation.15 | convolution fusion | flops 1258291200 | bytes 13844480 | tf_op jit(solution)/shard_map/mkr,rmc->mkc/dot_general | solution.py:36
  424.2 127.8 %all-reduce.3.cloned.1.call-done = f32[1,32,5120]{2,1,0:T(8,128)} async-done(((f32[1,32,5120]{2,1,0:T(8,128)}), f32[1,32,5120]{2,1,0:T(8,128)}) %all-reduce.3.cloned.1.call-update) | async-done | bytes 655376 | tf_op jit(solution)/shard_map/psum | solution.py:37
  552.0 11.1 %fusion.20 = f32[640,1,32]{0,2,1:T(8,128)} fusion(f32[1,640,1,5120]{1,3,2,0:T(8,128)} %copy-done.1, f32[1,32,5120]{2,1,0:T(8,128)} %all-reduce.3.cloned.1.call-done), kind=kOutput, calls=%fused_computation.19 | convolution fusion | flops 1258455040 | bytes 13844480 | tf_op jit(solution)/shard_map/rmc,mkc->rmk/dot_general | solution.py:27
  563.2 57.3 %all-gather.8.cloned.1.call-done = f32[20480,1,32]{0,2,1:T(8,128)} async-done(((f32[640,1,32]{0,2,1:T(8,128)}), f32[20480,1,32]{0,2,1:T(8,128)}) %all-gather.8.cloned.1.call-update) | async-done | bytes 2621456 | tf_op jit(solution)/shard_map/all_gather | solution.py:28
  620.5 3.3 reshape.196
  623.8 2.5 reduce_sum.34
  626.4 2.1 fusion.46
  628.4 1.1 broadcast_multiply_fusion.1
  629.7 2.9 custom-call.10
  632.6 0.6 compare_reduce_fusion
  633.2 0.7 fusion.35
  633.9 2.4 custom-call.11
  636.3 0.3 fusion.28
  636.6 17.9 %fusion.13 = f32[1,32,5120]{2,1,0:T(8,128)} fusion(f32[32,640]{1,0:T(8,128)S(1)} %fusion.28, f32[1,640,1,5120]{1,3,2,0:T(8,128)} %copy-done.1), kind=kOutput, calls=%fused_computation.16 | convolution fusion | flops 1258291200 | bytes 13844480 | tf_op jit(solution)/shard_map/mkr,rmc->mkc/dot_general | solution.py:36
  654.6 127.8 %all-reduce.5.cloned.1.call-done = f32[1,32,5120]{2,1,0:T(8,128)} async-done(((f32[1,32,5120]{2,1,0:T(8,128)}), f32[1,32,5120]{2,1,0:T(8,128)}) %all-reduce.5.cloned.1.call-update) | async-done | bytes 655376 | tf_op jit(solution)/shard_map/psum | solution.py:37
  782.3 1.1 broadcast_multiply_fusion
  783.5 11.1 %convolution_bitcast_fusion = f32[640,1,5120]{0,2,1:T(8,128)S(1)} fusion(f32[32,640]{1,0:T(8,128)S(1)} %fusion.28, f32[1,32,5120]{2,1,0:T(8,128)S(1)} %broadcast_multiply_fusion), kind=kOutput, calls=%fused_computation.14 | convolution fusion | flops 1258291200 | bytes 13844480 | tf_op jit(solution)/shard_map/mkr,mkc->rmc/dot_general | solution.py:38
  794.7 4.7 copy-done.2
  799.3 14.5 %fusion.1 = f32[1,640,1,5120]{1,3,2,0:T(8,128)} fusion(f32[640,1,5120]{0,2,1:T(8,128)S(1)} %convolution_bitcast_fusion, f32[1,640,1,5120]{1,3,2,0:T(8,128)} %copy.27, f32[640,5120]{0,1:T(8,128)} %convert_reduce_fusion), kind=kLoop, calls=%fused_computation.4 | loop fusion | flops 6553600 | bytes 52428800 | tf_op jit(solution)/shard_map/broadcast_in_dim | solution.py:39
  813.8 27.0 %copy.33 = f32[640,1,5120]{2,1,0:T(1,128)} copy(f32[640,1,5120]{0,2,1:T(8,128)} %copy-done.2) | data formatting | bytes 26214400
  840.9 27.0 %copy.34 = f32[1,640,1,5120]{3,2,1,0:T(1,128)} copy(f32[1,640,1,5120]{1,3,2,0:T(8,128)} %fusion.1) | data formatting | bytes 26214400
  (21 shorter events, 0.5 us)
Async XLA Ops:
  7.2 318.7 %copy-start = (f32[1,32,5120]{2,1,0:T(8,128)S(1)}, f32[1,32,5120]{2,1,0:T(8,128)}, u32[]{:S(2)}) copy-start(f32[1,32,5120]{2,1,0:T(8,128)} %param.10) | copy-start | bytes 1966084
  7.2 254.4 %all-gather.4.cloned.1.call-start = ((), (), s32[]{:S(2)}) async-start(), calls=%async_computation.1 | async-start | bytes 17694720 | tf_op jit(solution)/shard_map/all_gather | solution.py:17
  53.7 85.3 %all-to-all-start = ((bf16[8,2,61440]{2,1,0:T(2,128)(2,1)}), bf16[8,2,61440]{2,1,0:T(2,128)(2,1)S(1)}, u32[]{:S(2)}, u32[]{:S(2)}) async-start(bf16[8,2,61440]{2,1,0:T(2,128)(2,1)} %reshape.206), calls=%async_computation | async-start | bytes 3932160 | tf_op jit(solution)/shard_map/all_to_all | solution.py:16
  61.0 329.4 %all-gather.6.cloned.1.call-start = ((), (), s32[]{:S(2)}) async-start(), calls=%async_computation.2 | async-start | bytes 2703360 | tf_op jit(solution)/shard_map/all_gather | solution.py:28
  321.2 4.7 copy-start.1
  333.8 218.1 %all-reduce.3.cloned.1.call-start = ((), (), s32[]{:S(2)}) async-start(), calls=%async_computation.3 | async-start | bytes 1310720 | tf_op jit(solution)/shard_map/psum | solution.py:37
  424.2 196.3 %all-gather.8.cloned.1.call-start = ((), (), s32[]{:S(2)}) async-start(), calls=%async_computation.4 | async-start | bytes 2703360 | tf_op jit(solution)/shard_map/all_gather | solution.py:28
  563.1 219.2 %all-reduce.5.cloned.1.call-start = ((), (), s32[]{:S(2)}) async-start(), calls=%async_computation.5 | async-start | bytes 1310720 | tf_op jit(solution)/shard_map/psum | solution.py:37
  783.5 30.3 %copy-start.3 = (f32[1,32,5120]{2,1,0:T(8,128)}, f32[1,32,5120]{2,1,0:T(8,128)S(1)}, u32[]{:S(2)}) copy-start(f32[1,32,5120]{2,1,0:T(8,128)S(1)} %broadcast_multiply_fusion) | copy-start | bytes 1966084
  794.6 4.7 copy-start.2
Sparse Core Ops, SparseCore 0:
  10.2 251.3 all-gather.3
  334.0 56.3 all-gather.5
  424.3 127.6 all-reduce.2
  563.3 57.1 all-gather.7
  654.7 127.6 all-reduce.4
where the time goes:
time: 885 us; the launch traced here: 875 us
  waiting for transfers between devices  533 us (60%)
  local copies, waits for them, and re-layouts  125 us (14%)
  other arithmetic  98.1 us (11%)
  matrix products  97.7 us (11%)
  between operations  14.4 us (2%)
    psum x2, waiting for transfers between devices, local(): right = lax.psum(right, ('grp', 'shard')) / groups  256 us
    unnamed x16, local copies, waits for them, and re-layouts  116 us
    all_gather x2, waiting for transfers between devices, local(): gathered = lax.all_gather(left, ('grp', 'shard'), axis=0, tiled=True)  114 us
    all_gather x1, waiting for transfers between devices, local(): piece = lax.all_gather(out_grads, 'shard', axis=1, tiled=True)  112 us
    all_to_all x1, waiting for transfers between devices, local(): lax.all_to_all(activations, 'shard', split_axis=2, concat_axis=1, tiled=T...  50.8 us
    dot_general x2, matrix products, local(): right = jnp.einsum('mkr,rmc->mkc', basis, momentum, precision=high)  35.6 us
    unnamed x1, other arithmetic  29.2 us
    dot_general x1, matrix products, local(): jnp.einsum('mkta,mktc->kamc', mine, grads, preferred_element_type=jnp.flo...  27.1 us
  transfers between devices with their start and end apart: 6, of which 6 were waited for; matrix products, arithmetic and copies ran while one was open for 10% of the time, Pallas kernels for 0%

commit v1 on v0

v1 whole, which is shorter than its diff:
```python
import functools

import jax
import jax.numpy as jnp
from jax import lax
from jax.experimental import pallas as pl
from jax.experimental.pallas import tpu as pltpu
from jax.sharding import PartitionSpec as P

ITERS = 2
CHUNKS = 4
LANES = 128
F32 = jnp.float32
BF16 = jnp.bfloat16
NN = (((1,), (0,)), ((), ()))
NT = (((1,), (1,)), ((), ()))


def split(x):
    high = x.astype(BF16)
    return high, (x - high.astype(F32)).astype(BF16)


def dot2(x, y, dims):
    rows = x.shape[0]
    both = lax.dot_general(jnp.concatenate(split(x), axis=0), y, dims, preferred_element_type=F32)
    return both[:rows] + both[rows:]


def dot3(x, y_high, y_low, dims):
    return dot2(x, y_high, dims) + lax.dot_general(x.astype(BF16), y_low, dims, preferred_element_type=F32)


def inverse_lower(gram):
    n = gram.shape[0]
    row = lax.broadcasted_iota(jnp.int32, (n, n), 0)
    col = lax.broadcasted_iota(jnp.int32, (n, n), 1)
    work = jnp.concatenate([gram, jnp.where(row == col, 1.0, 0.0).astype(F32)], axis=1)
    below = lax.broadcasted_iota(jnp.int32, (n, 1), 0)
    for j in range(n):
        pivot = work[j:j + 1, :]
        scaled = pivot * lax.rsqrt(work[j:j + 1, j:j + 1])
        column = work[:, j:j + 1] * lax.rsqrt(work[j:j + 1, j:j + 1])
        work = jnp.where(below > j, work - column * scaled, jnp.where(below == j, scaled, work))
    return work[:, n:]


def exchange_kernel(groups, shards, sizes, act_ref, grad_ref, err_ref, q_ref,
                    all_ref, cols_ref, basis_ref, factor_ref,
                    a_send, e_high, e_low, e_buf, w_buf, l_buf, m_buf, z_send, z_buf, r_send, r_buf, s_send, s_buf, f_buf, x_buf,
                    sem_local, sem_e, sem_up, sem_down, sem_side, sem_block, *sems):
    zs, ys = sizes
    me, grp = lax.axis_index("shard"), lax.axis_index("grp")
    z, y = me // ys, me % ys
    tok, width = grad_ref.shape
    own = width // shards
    rank = q_ref.shape[0]
    part = rank // groups
    tiles = width // LANES
    step_rows = tok // CHUNKS

    barrier = pltpu.get_barrier_semaphore()
    for k in range(1, shards):
        pl.semaphore_signal(barrier, inc=1, device_id={"shard": (me + k) % shards}, device_id_type=pl.DeviceIdType.MESH)
    for k in range(1, groups):
        pl.semaphore_signal(barrier, inc=1, device_id={"grp": (grp + k) % groups}, device_id_type=pl.DeviceIdType.MESH)

    err_rows = e_buf.shape[1] // tiles
    loads = own // err_rows

    def err_copy(i, slot):
        return pltpu.make_async_copy(err_ref.at[pl.ds(i * err_rows * tiles, err_rows * tiles), :], e_buf.at[slot], sem_e.at[slot])

    err_copy(0, 0).start()

    for t in range(shards):
        a_send[t] = act_ref[:, t * own:(t + 1) * own]

    pl.semaphore_wait(barrier, shards - 1 + groups - 1)

    pending = []

    def send(axis, src, dst, send_sem, recv_sem, target):
        copy = pltpu.make_async_remote_copy(src_ref=src, dst_ref=dst, send_sem=send_sem, recv_sem=recv_sem,
                                            device_id={axis: target}, device_id_type=pl.DeviceIdType.MESH)
        return copy

    def spread(axis, count, index, src, buf, ssem, rsem):
        for k in range(1, count):
            target = (index + k) % count
            copy = send(axis, src(target), buf.at[index], ssem.at[k], rsem.at[k], target)
            copy.start()
            pending.append(copy)

    def collect(axis, count, index, buf, ssem, rsem):
        for k in range(1, count):
            slot = buf.at[(index + count - k) % count]
            send(axis, slot, slot, ssem.at[k], rsem.at[k], (index + k) % count).wait_recv()

    spread("shard", shards, me, lambda t: a_send.at[t], cols_ref, sems[0], sems[1])
    own_cols = pltpu.make_async_copy(a_send.at[me], cols_ref.at[me], sem_local.at[0])
    own_cols.start()

    def piece(c):
        return pl.ds(c * step_rows, step_rows)

    def block(owner, c):
        return all_ref.at[owner, piece(c), :]

    def up(owner, zsrc, c, src):
        return send("shard", src, block(owner, c), sem_up.at[zsrc, c], sem_block.at[owner, c], (z + 1) * ys + y)

    def down(owner, zsrc, c, src):
        return send("shard", src, block(owner, c), sem_down.at[zsrc, c], sem_block.at[owner, c], (z - 1) * ys + y)

    def side(owner, zsrc, c, src, k):
        return send("shard", src, block(owner, c), sem_side.at[k, zsrc, c], sem_block.at[owner, c], z * ys + (y + k) % ys)

    own_block = pltpu.make_async_copy(grad_ref, all_ref.at[me], sem_local.at[1])
    own_block.start()
    for c in range(CHUNKS):
        src = grad_ref.at[piece(c), :]

        @pl.when(z + 1 < zs)
        def _():
            up(me, z, c, src).start()

        @pl.when(z > 0)
        def _():
            down(me, z, c, src).start()

        for k in range(1, ys):
            side(me, z, c, src, k).start()

    def forward(step, c):
        @pl.when(z >= step)
        def _():
            zsrc = z - step
            owner = zsrc * ys + y
            up(owner, zsrc, c, block(owner, c)).wait_recv()

            @pl.when(z + 1 < zs)
            def _():
                up(owner, zsrc, c, block(owner, c)).start()

            for k in range(1, ys):
                side(owner, zsrc, c, block(owner, c), k).start()

        @pl.when(z + step < zs)
        def _():
            zsrc = z + step
            owner = zsrc * ys + y
            down(owner, zsrc, c, block(owner, c)).wait_recv()

            @pl.when(z > 0)
            def _():
                down(owner, zsrc, c, block(owner, c)).start()

            for k in range(1, ys):
                side(owner, zsrc, c, block(owner, c), k).start()

    events = [(step, c) for step in range(1, zs) for c in range(CHUNKS)]

    def advance(count):
        for _ in range(min(count, len(events))):
            forward(*events.pop(0))

    def load_step(i, slot):
        err_copy(i, slot).wait()

        @pl.when(i + 1 < loads)
        def _():
            err_copy(i + 1, 1 - slot).start()

        for t in range(tiles):
            high, low = split(e_buf[slot, pl.ds(t, err_rows, stride=tiles), :])
            rows = pl.ds(pl.multiple_of(i * err_rows, err_rows), err_rows)
            e_high[rows, t * LANES:(t + 1) * LANES] = high
            e_low[rows, t * LANES:(t + 1) * LANES] = low

    def load_body(i, carry):
        load_step(2 * i, 0)
        load_step(2 * i + 1, 1)
        return carry

    lax.fori_loop(0, loads // 2, load_body, 0)

    right = q_ref[...]
    for it in range(ITERS):
        sem = sems[2 + 14 * it:]
        w_buf[it, me] = dot2(right, grad_ref[...], NT)
        spread("shard", shards, me, lambda t: w_buf.at[it, me], w_buf.at[it], sem[0], sem[1])
        left = dot3(right, e_high[...], e_low[...], NT)
        if it == 0:
            own_cols.wait()
            collect("shard", shards, me, cols_ref, sems[0], sems[1])
        else:
            advance(1)
        collect("shard", shards, me, w_buf.at[it], sem[0], sem[1])
        for t in range(shards):
            left = left + dot2(w_buf[it, t], cols_ref[t], NN)
        l_buf[it, grp] = left
        spread("grp", groups, grp, lambda t: l_buf.at[it, grp], l_buf.at[it], sem[2], sem[3])
        advance(1)
        collect("grp", groups, grp, l_buf.at[it], sem[2], sem[3])
        left = l_buf[it, 0]
        for t in range(1, groups):
            left = left + l_buf[it, t]
        left = left * (1.0 / groups)
        m_buf[it, me] = lax.dot_general(left, left, NT, precision=lax.Precision.HIGHEST, preferred_element_type=F32)
        spread("shard", shards, me, lambda t: m_buf.at[it, me], m_buf.at[it], sem[4], sem[5])
        advance(1)
        collect("shard", shards, me, m_buf.at[it], sem[4], sem[5])
        gram = m_buf[it, 0]
        for t in range(1, shards):
            gram = gram + m_buf[it, t]
        basis = lax.dot_general(inverse_lower(gram), left, NN, precision=lax.Precision.HIGHEST, preferred_element_type=F32)
        for t in range(shards):
            z_send[it, t] = dot2(basis, cols_ref[t], NT)
        z_buf[it, me] = z_send[it, me]
        spread("shard", shards, me, lambda t: z_send.at[it, t], z_buf.at[it], sem[6], sem[7])
        advance(1)
        out = dot3(basis, e_high[...], e_low[...], NN)
        collect("shard", shards, me, z_buf.at[it], sem[6], sem[7])
        mine = z_buf[it, 0]
        for t in range(1, shards):
            mine = mine + z_buf[it, t]
        out = out + dot2(mine, grad_ref[...], NN)
        for t in range(groups):
            r_send[it, t] = out[t * part:(t + 1) * part, :]
        r_buf[it, grp] = r_send[it, grp]
        spread("grp", groups, grp, lambda t: r_send.at[it, t], r_buf.at[it], sem[8], sem[9])
        advance(1)
        collect("grp", groups, grp, r_buf.at[it], sem[8], sem[9])
        total = r_buf[it, 0]
        for t in range(1, groups):
            total = total + r_buf[it, t]
        for t in range(shards):
            s_send[it, t] = total[:, t * own:(t + 1) * own]
        s_buf[it, me] = s_send[it, me]
        spread("shard", shards, me, lambda t: s_send.at[it, t], s_buf.at[it], sem[10], sem[11])
        advance(1)
        collect("shard", shards, me, s_buf.at[it], sem[10], sem[11])
        total = s_buf[it, 0]
        for t in range(1, shards):
            total = total + s_buf[it, t]
        f_buf[it, me] = total * (1.0 / groups)
        spread("shard", shards, me, lambda t: f_buf.at[it, me], f_buf.at[it], sem[12], sem[13])
        collect("shard", shards, me, f_buf.at[it], sem[12], sem[13])
        for t in range(shards):
            x_buf[it, grp, :, t * own:(t + 1) * own] = f_buf[it, t]
        gsem = sems[2 + 14 * ITERS + 2 * it:]
        spread("grp", groups, grp, lambda t: x_buf.at[it, grp], x_buf.at[it], gsem[0], gsem[1])
        collect("grp", groups, grp, x_buf.at[it], gsem[0], gsem[1])
        right = jnp.concatenate([x_buf[it, t] for t in range(groups)], axis=0)
    basis_ref[...] = basis
    factor_ref[...] = right

    advance(len(events))
    own_block.wait()
    for k in range(1, ys):
        for zsrc in range(zs):
            for c in range(CHUNKS):
                owner = zsrc * ys + (y + k) % ys
                side(owner, zsrc, c, block(owner, c), k).wait_recv()
    for copy in pending:
        copy.wait_send()
    for c in range(CHUNKS):
        for zsrc in range(zs):
            owner = zsrc * ys + y
            src = block(owner, c)

            @pl.when((z + 1 < zs) & (zsrc <= z))
            def _():
                up(owner, zsrc, c, src).wait_send()

            @pl.when((z > 0) & (zsrc >= z))
            def _():
                down(owner, zsrc, c, src).wait_send()

            for k in range(1, ys):
                side(owner, zsrc, c, src, k).wait_send()


def finish_kernel(cols_ref, all_ref, err_ref, basis_ref, factor_ref, update_ref, next_ref, turned, turned_basis):
    own = turned.shape[0]
    count = err_ref.shape[0] // own

    @pl.when(pl.program_id(0) == 0)
    def _():
        turned[...] = cols_ref[...].T
        high, low = split(basis_ref[...].T)
        turned_basis[...] = jnp.concatenate([high, low, high], axis=1)

    high, low = split(factor_ref[...])
    update = lax.dot_general(turned_basis[...], jnp.concatenate([high, high, low], axis=0), NN, preferred_element_type=F32)
    gradient = lax.dot_general(turned[...], all_ref[...], NN, preferred_element_type=F32)
    rest = gradient - update
    for j in range(count):
        at = pl.ds(j, own, stride=count)
        lanes = slice(j * LANES, (j + 1) * LANES)
        update_ref[at, :] = update[:, lanes]
        next_ref[at, :] = err_ref[at, :] + rest[:, lanes]


def finish_block(cols_ref, all_ref, err_ref, basis_ref, factor_ref, update_ref, next_ref, turned, turned_basis):
    flat = lambda ref: ref.reshape(ref.shape[0] * ref.shape[1], LANES)
    finish_kernel(cols_ref, all_ref, flat(err_ref), basis_ref, factor_ref, flat(update_ref), flat(next_ref), turned, turned_basis)


def local(groups, shards, activations, out_grads, error, q_start):
    tok, width = activations.shape[1:]
    own = error.shape[1]
    rank = q_start.shape[1]
    tiles = width // LANES
    ys = 1
    while (2 * ys) ** 2 <= shards and shards % (2 * ys) == 0:
        ys *= 2
    zs = shards // ys
    part = rank // groups
    dma = pltpu.SemaphoreType.DMA
    stages = [shards] * 2
    for _ in range(ITERS):
        stages += [shards] * 2 + [groups] * 2 + [shards] * 4 + [groups] * 2 + [shards] * 4
    for _ in range(ITERS):
        stages += [groups] * 2
    vmem = pl.BlockSpec(memory_space=pltpu.VMEM)
    hbm = pl.BlockSpec(memory_space=pl.ANY)
    err_flat = error.reshape(own * tiles, LANES)
    gathered, cols, basis, factor = pl.pallas_call(
        functools.partial(exchange_kernel, groups, shards, (zs, ys)),
        out_shape=(
            jax.ShapeDtypeStruct((shards, tok, width), BF16),
            jax.ShapeDtypeStruct((shards, tok, own), BF16),
            jax.ShapeDtypeStruct((rank, own), F32),
            jax.ShapeDtypeStruct((rank, width), F32),
        ),
        in_specs=[vmem, vmem, hbm, vmem],
        out_specs=(hbm, vmem, vmem, vmem),
        scratch_shapes=[
            pltpu.VMEM((shards, tok, own), BF16),
            pltpu.VMEM((own, width), BF16),
            pltpu.VMEM((own, width), BF16),
            pltpu.VMEM((2, 32 * tiles, LANES), F32),
            pltpu.VMEM((ITERS, shards, rank, tok), F32),
            pltpu.VMEM((ITERS, groups, rank, own), F32),
            pltpu.VMEM((ITERS, shards, rank, rank), F32),
            pltpu.VMEM((ITERS, shards, rank, tok), F32),
            pltpu.VMEM((ITERS, shards, rank, tok), F32),
            pltpu.VMEM((ITERS, groups, part, width), F32),
            pltpu.VMEM((ITERS, groups, part, width), F32),
            pltpu.VMEM((ITERS, shards, part, own), F32),
            pltpu.VMEM((ITERS, shards, part, own), F32),
            pltpu.VMEM((ITERS, shards, part, own), F32),
            pltpu.VMEM((ITERS, groups, part, width), F32),
            dma((2,)),
            dma((2,)),
            dma((zs, CHUNKS)),
            dma((zs, CHUNKS)),
            dma((ys, zs, CHUNKS)),
            dma((shards, CHUNKS)),
        ] + [dma((count,)) for count in stages],
        compiler_params=pltpu.CompilerParams(collective_id=0, has_side_effects=True, vmem_limit_bytes=56 * 2 ** 20),
    )(activations[0], out_grads[0], err_flat, q_start[0])

    span = 8 if tiles % 8 == 0 else tiles
    tokens = shards * tok
    update, error_next = pl.pallas_call(
        finish_block,
        grid=(tiles // span,),
        out_shape=(jax.ShapeDtypeStruct((own, tiles, LANES), F32),) * 2,
        in_specs=[
            pl.BlockSpec((tokens, own), lambda i: (0, 0)),
            pl.BlockSpec((tokens, span * LANES), lambda i: (0, i)),
            pl.BlockSpec((own, span, LANES), lambda i: (0, i, 0)),
            pl.BlockSpec((rank, own), lambda i: (0, 0)),
            pl.BlockSpec((rank, span * LANES), lambda i: (0, i)),
        ],
        out_specs=(pl.BlockSpec((own, span, LANES), lambda i: (0, i, 0)),) * 2,
        scratch_shapes=[pltpu.VMEM((own, tokens), BF16), pltpu.VMEM((own, 3 * rank), BF16)],
        compiler_params=pltpu.CompilerParams(vmem_limit_bytes=56 * 2 ** 20),
    )(cols.reshape(tokens, own), gathered.reshape(tokens, width), error.reshape(own, tiles, LANES), basis, factor)
    return update.reshape(own, 1, width), error_next.reshape(1, own, 1, width), factor[None]


def solution(mesh):
    in_specs = (
        P(None, ("grp", "shard"), None),
        P(None, ("grp", "shard"), None),
        P("grp", "shard", None, None),
        P(),
    )
    out_specs = (P("shard", None, None), P("grp", "shard", None, None), P())
    body = functools.partial(local, mesh.shape["grp"], mesh.shape["shard"])
    return jax.shard_map(body, mesh=mesh, in_specs=in_specs, out_specs=out_specs, check_vma=False)
```

time: 885 us -> 336 us (0.38)
  waiting for transfers between devices: 533 us -> 0 us
  Pallas kernels: 0 us -> 331 us
  local copies, waits for them, and re-layouts: 125 us -> 0.84 us
  other arithmetic: 98.1 us -> 0 us
  matrix products: 97.7 us -> 0 us
  between operations: 14.4 us -> 0.65 us
    pallas_call x0 -> x2, Pallas kernels: none -> 331 us  [the longest x1 304 us: local(): pl.pallas_call(functools.partial(exchange_kernel, groups, shards, (zs, ys...]
    psum x2 -> x0, waiting for transfers between devices: 256 us -> none  [local(): right = lax.psum(right, ('grp', 'shard')) / groups]
    all_gather x3 -> x0, waiting for transfers between devices: 225 us -> none  [the longest x2 114 us: local(): gathered = lax.all_gather(left, ('grp', 'shard'), axis=0, tiled=True)]
    unnamed x16 -> x3, local copies, waits for them, and re-layouts: 116 us -> 0.84 us
    dot_general x8 -> x0, matrix products: 97 us -> none  [the longest x2 35.6 us: local(): right = jnp.einsum('mkr,rmc->mkc', basis, momentum, precision=high)]
    all_to_all x1 -> x0, waiting for transfers between devices: 50.8 us -> none  [local(): lax.all_to_all(activations, 'shard', split_axis=2, concat_axis=1, tiled=T...]
    unnamed x1 -> x0, other arithmetic: 29.2 us -> none
    reduce_sum x3 -> x0, other arithmetic: 27.8 us -> none  [the longest x1 22.8 us: local(): gradient = jnp.sum(rounded, axis=0)]
  transfers between devices with their start and end apart: 6 -> 0, of which waited for: 6 -> 0; matrix products, arithmetic and copies ran while one was open for 10% -> 0% of each run, Pallas kernels for 0% -> 0%
where the time goes in v1:
time: 336 us; the launch traced here: 333 us
  Pallas kernels  331 us (99%)
    pallas_call x1, Pallas kernels, local(): pl.pallas_call(functools.partial(exchange_kernel, groups, shards, (zs, ys...  304 us
    pallas_call x1, Pallas kernels, local(): pl.pallas_call(finish_block, grid=(tiles // span,), out_shape=(jax.ShapeD...  27.1 us

profile of v1, /device:TPU:0, one launch (start us, length us, event | category | flops | bytes accessed | tf_op | source)
XLA Modules:
  0.0 332.5 jit_solution(3549488956244134464)
XLA Ops:
  0.6 303.9 %shard_map.67 = (bf16[8,192,5120]{2,1,0:T(8,128)(2,1)}, bf16[8,192,640]{2,1,0:T(8,128)(2,1)}, f32[32,640]{1,0:T(8,128)}, f32[32,5120]{1,0:T(8,128)}) custom-call(bf16[192,5120]{1,0:T(8,128)(2,1)} %bitcast.14, bf16[192,5120]{1,0:T(8,128)(2,1)} %bitcast.15, f32[25600,128]{1,0:T(8,128)} %bitcast.10, f32[32,5120]{1,0:T(8,128)} %bitcast.17), custom_call_target="tpu_custom_call" | custom-call | tf_op jit(solution)/shard_map/pallas_call | solution.py:330
  304.6 0.0 copy-start
  304.6 27.1 %shard_map.68 = (f32[640,40,128]{2,1,0:T(8,128)}, f32[640,40,128]{2,1,0:T(8,128)}) custom-call(bf16[1536,640]{1,0:T(8,128)(2,1)} %bitcast.16, bf16[1536,5120]{1,0:T(8,128)(2,1)} %bitcast.12, f32[640,40,128]{2,1,0:T(8,128)} %bitcast.11, f32[32,640]{1,0:T(8,128)} %get-tuple-element.11.basis_ref, f32[32,5120]{1,0:T(8,128)} %get-tuple-element.12.factor_ref), custom_call_target="tpu_custom_call" | custom-call | tf_op jit(solution)/shard_map/pallas_call | solution.py:368
  331.7 0.0 copy-done
  331.7 0.8 copy.10
Async XLA Ops:
  304.6 27.1 %copy-start = (f32[32,5120]{1,0:T(8,128)S(1)}, f32[32,5120]{1,0:T(8,128)}, u32[]{:S(2)}) copy-start(f32[32,5120]{1,0:T(8,128)} %get-tuple-element.12.factor_ref) | copy-start | bytes 1966084
